TPU v7x, 512 devices: a whole 4x4x16 slice. The times are simulated.
512 devices in a mesh: ka: 8 (over x, core), pts: 64 (over z, y).
Axes of the slice: x: 4, y: 4, z: 16, core: 2. Of those that a mesh axis runs over, the one named last changes fastest.
Arguments:
- orbitals: bfloat16 [216, 2, 4096, 384], P('ka', None, 'pts'), may hold values from -1.5 to 1.5
- counts: int32 [216], P('ka'), may hold values from 60 to 300
- occupation: float32 [216, 384], P('ka'), may hold values from 0.2 to 1
- coulomb: bfloat16 [216, 2, 64, 4096], P('ka', None, None, 'pts'), may hold values from -24 to 24
Outputs:
- exchange_block: bfloat16 [216, 2, 64, 4096], P('ka', None, None, 'pts')
Inputs may be any that keep to these rules, and one draw needn't show every extreme that they name: `counts`: between 60 and 300 occupied bands per k-point.
All inputs are finite; a program needn't handle non-finite values.
Results may differ from a plain program's by a relative error of at most 0.0057.
Values may be sent and summed in bfloat16 or wider, within the bound.
A program may use at most 64 MiB of HBM per device.

v0:
```python
import jax
import jax.numpy as jnp
from jax import lax
from jax.sharding import Mesh
from jax.sharding import PartitionSpec as P

KSIDE = 6
ROW_DEV = 1
PTS = ("pts_0", "pts_1")
KA = ("ka_0", "ka_1")


def gather_axes(array, axes, dim):
    for axis in reversed(axes):
        array = lax.all_gather(array, axis, axis=dim, tiled=True)
    return array


def split_up(array, dim, devices):
    before, after = (array.shape[:dim], array.shape[dim + 1 :])
    return jnp.moveaxis(array.reshape(*before, devices, -1, *after), dim, 0)


def in_order(parts, dim):
    parts = jnp.moveaxis(parts, 0, dim)
    dims = parts.shape
    return parts.reshape(*dims[:dim], dims[dim] * dims[dim + 1], *dims[dim + 2 :])


def moved_by_axis(parts, axes, turns):
    inside = parts.shape[1:]
    whole = parts.reshape(*(lax.axis_size(a) for a in axes), *inside)
    for k in turns:
        whole = lax.all_to_all(whole, axes[k], k, k, tiled=True)
    return whole.reshape(-1, *inside)


def exchange_by_axis(array, axes, turns, split_dim, concat_dim):
    parts = split_up(array, split_dim, lax.axis_size(axes))
    return in_order(moved_by_axis(parts, axes, turns), concat_dim)


def band_gram(left, right):

    def product(first, second):
        return jnp.einsum("krb,knb->krn", first, second, preferred_element_type=jnp.float32)

    real = product(left[:, 0], right[:, 0]) + product(left[:, 1], right[:, 1])
    imag = product(left[:, 1], right[:, 0]) - product(left[:, 0], right[:, 1])
    return jnp.stack([real, imag], 1)


def side_table(sign):
    index = jnp.arange(KSIDE, dtype=jnp.int32)
    phase = index[:, None] * index[None, :] % KSIDE
    angle = phase.astype(jnp.float32) * (2.0 * jnp.pi / KSIDE)
    cosine = jnp.cos(angle)
    sine = jnp.sin(angle) * sign
    top = jnp.stack([cosine, sine], 2)
    bottom = jnp.stack([-sine, cosine], 2)
    return jnp.stack([top, bottom], 1)


def mesh_transform(values, sign):
    table = side_table(sign)
    forms = ["acbd,bxydm->axycm", "acbd,xbydm->xaycm", "acbd,xybdm->xyacm"]
    for form in forms:
        values = jnp.einsum(
            form, table, values, precision=lax.Precision.HIGHEST, preferred_element_type=jnp.float32
        )
    return values


def convolve(density, kernel):
    shape = density.shape
    count = shape[0]
    dens = mesh_transform(density.astype(jnp.float32).reshape(KSIDE, KSIDE, KSIDE, 2, -1), 1.0)
    kern = mesh_transform(kernel.astype(jnp.float32).reshape(KSIDE, KSIDE, KSIDE, 2, -1), 1.0)
    prod_re = kern[:, :, :, 0] * dens[:, :, :, 0] - kern[:, :, :, 1] * dens[:, :, :, 1]
    prod_im = kern[:, :, :, 0] * dens[:, :, :, 1] + kern[:, :, :, 1] * dens[:, :, :, 0]
    back = mesh_transform(jnp.stack([prod_re, prod_im], 3), -1.0)
    scale = -1.0 / (count * count)
    return (back * scale).reshape(shape).astype(jnp.bfloat16)


def local(orbitals, counts, occupation, coulomb):
    slots = orbitals.shape[3]
    band = jnp.arange(slots, dtype=jnp.int32)
    weights = jnp.where(band[None, :] < counts[:, None], occupation, jnp.float32(0.0))
    weighted = (orbitals[:, :, :ROW_DEV, :].astype(jnp.float32) * weights[:, None, None, :]).astype(
        jnp.bfloat16
    )
    gathered = gather_axes(weighted, PTS, 2)
    density = band_gram(gathered, orbitals).astype(jnp.bfloat16)
    result = convolve(
        lax.all_to_all(density, KA, split_axis=3, concat_axis=0, tiled=True),
        lax.all_to_all(coulomb, KA, split_axis=3, concat_axis=0, tiled=True),
    )
    return exchange_by_axis(result, KA, (1, 0), 0, 3)


def solution(mesh):
    finer = Mesh(mesh.devices.reshape(4, 2, 16, 4), ("ka_0", "ka_1", "pts_0", "pts_1"))
    in_specs = (P(KA, None, PTS, None), P(KA), P(KA, None), P(KA, None, None, PTS))
    out_specs = P(KA, None, None, PTS)
    return jax.shard_map(local, mesh=finer, in_specs=in_specs, out_specs=out_specs, check_vma=False)
```

profile of v0, /device:TPU:1, one launch (start us, length us, event | category | flops | bytes accessed | tf_op | source)
XLA Modules:
  0.0 193.9 jit_solution(1851961340840522494)
XLA Ops:
  6.5 1.0 slice.36
  7.6 0.9 fusion.43
  8.5 11.3 %all_gather.6 = bf16[27,2,4,384]{3,1,0,2:T(2,128)(2,1)} all-gather(bf16[27,2,1,384]{3,1,0,2:T(2,128)(2,1)S(1)} %multiply_convert_fusion), channel_id=1, replica_groups=mesh['ka_0'=4,'ka_1'=2,'pts_0'=16,'pts_1'=4] {'pts_1'}, dimensions={2}, use_global_device_ids=true | all-gather | bytes 207360 | tf_op jit(solution)/shard_map/all_gather | solution.py:15
  19.8 2.4 %copy.57 = bf16[27,2,64,64]{2,1,0,3:T(2,128)(2,1)S(1)} copy(bf16[27,2,64,64]{3,2,1,0:T(8,128)(2,1)} %param.7) | data formatting | bytes 884736 | tf_op args[3]
  22.2 1.3 reshape.130
  23.5 11.8 %all-to-all-start = ((bf16[8,2,13824]{2,1,0:T(2,128)(2,1)}), bf16[8,2,13824]{2,1,0:T(2,128)(2,1)S(1)}, u32[]{:S(2)}, u32[]{:S(2)}) async-start(bf16[8,2,13824]{2,1,0:T(2,128)(2,1)} %reshape.130), calls=%async_computation | async-start | bytes 884736 | tf_op jit(solution)/shard_map/all_to_all | solution.py:97
  35.7 8.2 %all-to-all-done = bf16[8,2,13824]{2,1,0:T(2,128)(2,1)S(1)} async-done(((bf16[8,2,13824]{2,1,0:T(2,128)(2,1)}), bf16[8,2,13824]{2,1,0:T(2,128)(2,1)S(1)}, u32[]{:S(2)}, u32[]{:S(2)}) %all-to-all-start) | async-done | bytes 442400 | tf_op jit(solution)/shard_map/all_to_all | solution.py:97
  43.9 0.5 reshape.131
  44.5 0.2 copy.158
  44.7 4.8 %copy.59 = bf16[8,27,2,64,8]{4,3,2,1,0:T(8,128)(2,1)} copy(bf16[8,27,2,64,8]{3,4,0,2,1:T(8,128)(2,1)S(1)} %bitcast.175) | data formatting | bytes 884736 | tf_op jit(solution)/shard_map/all_to_all | solution.py:97
  49.5 9.7 %reshape.104 = bf16[6,6,6,2,512]{4,3,2,1,0:T(2,128)(2,1)S(1)} reshape(bf16[8,27,2,64,8]{4,3,2,1,0:T(8,128)(2,1)} %copy.59) | data formatting | bytes 884736 | tf_op jit(solution)/shard_map/reshape | solution.py:78
  59.2 1.1 convolution_bitcast_fusion.8
  60.3 32.4 %all-gather.2.cloned.1.call-done = bf16[27,2,64,384]{3,1,0,2:T(2,128)(2,1)} async-done(((bf16[27,2,4,384]{3,1,0,2:T(2,128)(2,1)}), bf16[27,2,64,384]{3,1,0,2:T(2,128)(2,1)}) %all-gather.2.cloned.1.call-update) | async-done | bytes 2654224 | tf_op jit(solution)/shard_map/all_gather | solution.py:15
  92.7 6.9 %fusion.63 = (bf16[27,1,64,384]{3,1,0,2:T(2,128)(2,1)S(1)}, bf16[27,1,64,384]{3,1,0,2:T(2,128)(2,1)S(1)}) fusion(bf16[27,2,64,384]{3,1,0,2:T(2,128)(2,1)} %all-gather.2.cloned.1.call-done), kind=kLoop, calls=%fused_computation.79 | loop fusion | bytes 5308416 | tf_op jit(solution)/shard_map/slice | solution.py:48
  99.7 0.6 fusion.3
  100.3 0.6 fusion.1
  100.9 0.6 fusion.23
  101.5 0.6 fusion.26
  102.1 0.2 pad_maximum_fusion
  102.3 0.8 copy.68
  103.1 1.3 reshape.128
  104.4 14.1 %all-to-all-start.1 = ((bf16[8,2,13824]{2,1,0:T(2,128)(2,1)}), bf16[8,2,13824]{2,1,0:T(2,128)(2,1)S(1)}, u32[]{:S(2)}, u32[]{:S(2)}) async-start(bf16[8,2,13824]{2,1,0:T(2,128)(2,1)} %reshape.128), calls=%async_computation.1 | async-start | bytes 884736 | tf_op jit(solution)/shard_map/all_to_all | solution.py:96
  118.5 1.9 convolution_bitcast_fusion.6
  120.5 1.8 convolution_bitcast_fusion.5
  122.2 4.9 %all-to-all-done.1 = bf16[8,2,13824]{2,1,0:T(2,128)(2,1)S(1)} async-done(((bf16[8,2,13824]{2,1,0:T(2,128)(2,1)}), bf16[8,2,13824]{2,1,0:T(2,128)(2,1)S(1)}, u32[]{:S(2)}, u32[]{:S(2)}) %all-to-all-start.1) | async-done | bytes 442400 | tf_op jit(solution)/shard_map/all_to_all | solution.py:96
  127.1 0.5 reshape.129
  127.7 0.2 copy.157
  127.9 4.8 %copy.70 = bf16[8,27,2,64,8]{4,3,2,1,0:T(8,128)(2,1)} copy(bf16[8,27,2,64,8]{3,4,0,2,1:T(8,128)(2,1)S(1)} %bitcast.176) | data formatting | bytes 884736 | tf_op jit(solution)/shard_map/all_to_all | solution.py:96
  132.7 9.7 %reshape.105 = bf16[6,6,6,2,512]{4,3,2,1,0:T(2,128)(2,1)S(1)} reshape(bf16[8,27,2,64,8]{4,3,2,1,0:T(8,128)(2,1)} %copy.70) | data formatting | bytes 884736 | tf_op jit(solution)/shard_map/reshape | solution.py:77
  142.4 0.8 convolution_bitcast_fusion.7
  143.2 1.9 convolution_bitcast_fusion.4
  145.1 1.8 convolution_bitcast_fusion.3
  146.9 0.3 multiply_subtract_fusion
  147.3 1.8 convolution_bitcast_fusion.2
  149.1 1.9 convolution_bitcast_fusion.1
  151.0 1.7 fusion.22
  152.7 0.3 copy.79
  153.0 9.4 %convert_element_type.66 = bf16[4,2,27,2,64,8]{5,4,3,2,1,0:T(8,128)(2,1)} reshape(bf16[6,6,6,2,512]{4,3,2,1,0:T(2,128)(2,1)S(1)} %copy.79) | data formatting | bytes 884736 | tf_op jit(solution)/shard_map/convert_element_type | solution.py:83
  162.4 5.5 %copy.80 = bf16[4,2,27,2,64,8]{4,5,3,2,0,1:T(8,128)(2,1)S(1)} copy(bf16[4,2,27,2,64,8]{5,4,3,2,1,0:T(8,128)(2,1)} %convert_element_type.66) | data formatting | bytes 884736 | tf_op jit(solution)/shard_map/convert_element_type | solution.py:83
  168.0 0.8 reshape.132
  168.7 4.6 %all_to_all.40 = bf16[2,2,55296]{2,1,0:T(2,128)(2,1)S(1)} all-to-all(bf16[2,2,55296]{2,1,0:T(2,128)(2,1)S(1)} %reshape.132), channel_id=1, replica_groups=mesh['ka_0'=4,'ka_1'=2,'pts_0'=16,'pts_1'=4] {'ka_1'}, dimensions={0} | all-to-all | bytes 884736 | tf_op jit(solution)/shard_map/all_to_all | solution.py:34
  173.3 0.7 reshape.133
  174.0 0.2 copy_bitcast_fusion.8
  174.1 0.5 reshape.134
  174.6 10.4 %all_to_all.41 = bf16[4,2,27648]{2,1,0:T(2,128)(2,1)S(1)} all-to-all(bf16[4,2,27648]{2,1,0:T(2,128)(2,1)S(1)} %reshape.134), channel_id=1, replica_groups=mesh['ka_0'=4,'ka_1'=2,'pts_0'=16,'pts_1'=4] {'ka_0'}, dimensions={0} | all-to-all | bytes 884736 | tf_op jit(solution)/shard_map/all_to_all | solution.py:34
  185.1 0.5 reshape.135
  185.6 0.2 copy.82
  185.8 1.2 copy.83
  (14 shorter events, 0.6 us)
Async XLA Ops:
  6.5 86.2 %all-gather.2.cloned.1.call-start = ((), (), s32[]{:S(2)}) async-start(), calls=%async_computation.4 | async-start | bytes 2820096 | tf_op jit(solution)/shard_map/all_gather | solution.py:15
  23.5 20.4 %all-to-all-start = ((bf16[8,2,13824]{2,1,0:T(2,128)(2,1)}), bf16[8,2,13824]{2,1,0:T(2,128)(2,1)S(1)}, u32[]{:S(2)}, u32[]{:S(2)}) async-start(bf16[8,2,13824]{2,1,0:T(2,128)(2,1)} %reshape.130), calls=%async_computation | async-start | bytes 884736 | tf_op jit(solution)/shard_map/all_to_all | solution.py:97
  92.7 6.9 %copy-start = (bf16[27,2,64,384]{3,2,1,0:T(8,128)(2,1)S(1)}, bf16[27,2,64,384]{3,2,1,0:T(8,128)(2,1)}, u32[]{:S(2)}) copy-start(bf16[27,2,64,384]{3,2,1,0:T(8,128)(2,1)} %param.4) | copy-start | bytes 7962628
  104.4 22.7 %all-to-all-start.1 = ((bf16[8,2,13824]{2,1,0:T(2,128)(2,1)}), bf16[8,2,13824]{2,1,0:T(2,128)(2,1)S(1)}, u32[]{:S(2)}, u32[]{:S(2)}) async-start(bf16[8,2,13824]{2,1,0:T(2,128)(2,1)} %reshape.128), calls=%async_computation.1 | async-start | bytes 884736 | tf_op jit(solution)/shard_map/all_to_all | solution.py:96
Sparse Core Ops, SparseCore 0:
  19.9 72.7 all-gather.1
where the time goes:
time: 195 us; the launch traced here: 194 us
  local copies, waits for them, and re-layouts  63.6 us (33%)
  waiting for transfers between devices  45.5 us (23%)
  blocking collectives  26.3 us (13%)
  starting transfers between devices  25.9 us (13%)
  matrix products  17.1 us (9%)
  between operations  13.7 us (7%)
    all_gather x1, waiting for transfers between devices, gather_axes(): array = lax.all_gather(array, axis, axis=dim, tiled=True)  32.4 us
    convert_element_type x3, local copies, waits for them, and re-layouts, convolve(): return (back * scale).reshape(shape).astype(jnp.bfloat16)  15.3 us
    all_to_all x2, blocking collectives, moved_by_axis(): whole = lax.all_to_all(whole, axes[k], k, k, tiled=True)  15 us
    dot_general x9, matrix products, mesh_transform(): jnp.einsum(form, table, values, precision=lax.Precision.HIGHEST, preferre...  14.7 us
    all_to_all x1, starting transfers between devices, local(): lax.all_to_all(density, KA, split_axis=3, concat_axis=0, tiled=True)  14.1 us
    all_to_all x1, starting transfers between devices, local(): lax.all_to_all(coulomb, KA, split_axis=3, concat_axis=0, tiled=True)  11.8 us
    all_gather x1, blocking collectives, gather_axes(): array = lax.all_gather(array, axis, axis=dim, tiled=True)  11.3 us
    reshape x1, local copies, waits for them, and re-layouts, convolve(): kernel.astype(jnp.float32).reshape(KSIDE, KSIDE, KSIDE, 2, -1)  9.7 us
  transfers between devices with their start and end apart: 3, of which 3 were waited for; matrix products, arithmetic and copies ran while one was open for 12% of the time, Pallas kernels for 0%

commit v1 on v0

--- a/solution.py
+++ b/solution.py
@@ -8,6 +8,13 @@
 ROW_DEV = 1
 PTS = ("pts_0", "pts_1")
 KA = ("ka_0", "ka_1")
+
+
+def exchange_blocks(array, mesh_axis, split, join):
+    count = lax.axis_size(mesh_axis)
+    parts = jnp.stack(jnp.split(array, count, axis=split), axis=0)
+    parts = lax.all_to_all(parts, mesh_axis, split_axis=0, concat_axis=0)
+    return jnp.concatenate(parts, axis=join)
 
 
 def gather_axes(array, axes, dim):
@@ -94,7 +101,7 @@
     density = band_gram(gathered, orbitals).astype(jnp.bfloat16)
     result = convolve(
         lax.all_to_all(density, KA, split_axis=3, concat_axis=0, tiled=True),
-        lax.all_to_all(coulomb, KA, split_axis=3, concat_axis=0, tiled=True),
+        exchange_blocks(coulomb, KA, 3, 0),
     )
     return exchange_by_axis(result, KA, (1, 0), 0, 3)
 

time: 195 us -> 195 us (level)
  local copies, waits for them, and re-layouts: 63.6 us -> 80.7 us
  waiting for transfers between devices: 45.5 us -> 29.2 us
    all_gather x1, waiting for transfers between devices: 32.4 us -> 16 us  [gather_axes(): array = lax.all_gather(array, axis, axis=dim, tiled=True)]
    unnamed x13 -> x36, local copies, waits for them, and re-layouts: 8.7 us -> 17.3 us
    split x0 -> x1, local copies, waits for them, and re-layouts: none -> 8.48 us  [exchange_blocks(): parts = jnp.stack(jnp.split(array, count, axis=split), axis=0)]
    all_to_all x2 -> x1, local copies, waits for them, and re-layouts: 5.02 us -> 4.82 us  [exchange_blocks(): parts = lax.all_to_all(parts, mesh_axis, split_axis=0, concat_axis=0)]
  transfers between devices with their start and end apart: 3 -> 3, of which waited for: 3 -> 3; matrix products, arithmetic and copies ran while one was open for 12% -> 21% of each run, Pallas kernels for 0% -> 0%
where the time goes in v1:
time: 195 us; the launch traced here: 194 us
  local copies, waits for them, and re-layouts  80.7 us (41%)
  waiting for transfers between devices  29.2 us (15%)
  blocking collectives  26.3 us (13%)
  starting transfers between devices  25.6 us (13%)
  matrix products  16.7 us (9%)
  between operations  13.8 us (7%)
    unnamed x36, local copies, waits for them, and re-layouts  17.3 us
    all_gather x1, waiting for transfers between devices, gather_axes(): array = lax.all_gather(array, axis, axis=dim, tiled=True)  16 us
    convert_element_type x3, local copies, waits for them, and re-layouts, convolve(): return (back * scale).reshape(shape).astype(jnp.bfloat16)  15.2 us
    all_to_all x2, blocking collectives, moved_by_axis(): whole = lax.all_to_all(whole, axes[k], k, k, tiled=True)  15 us
    dot_general x9, matrix products, mesh_transform(): jnp.einsum(form, table, values, precision=lax.Precision.HIGHEST, preferre...  14.2 us
    all_to_all x1, starting transfers between devices, local(): lax.all_to_all(density, KA, split_axis=3, concat_axis=0, tiled=True)  13.8 us
    all_to_all x1, starting transfers between devices, exchange_blocks(): parts = lax.all_to_all(parts, mesh_axis, split_axis=0, concat_axis=0)  11.8 us
    all_gather x1, blocking collectives, gather_axes(): array = lax.all_gather(array, axis, axis=dim, tiled=True)  11.3 us
  transfers between devices with their start and end apart: 3, of which 3 were waited for; matrix products, arithmetic and copies ran while one was open for 21% of the time, Pallas kernels for 0%

profile of v1, /device:TPU:1, one launch (start us, length us, event | category | flops | bytes accessed | tf_op | source)
XLA Modules:
  0.0 194.1 jit_solution(13398385323474761805)
XLA Ops:
  6.5 1.0 slice.36
  7.6 0.9 fusion.42
  8.5 11.3 %all_gather.6 = bf16[27,2,4,384]{3,1,0,2:T(2,128)(2,1)} all-gather(bf16[27,2,1,384]{3,1,0,2:T(2,128)(2,1)S(1)} %multiply_convert_fusion), channel_id=1, replica_groups=mesh['ka_0'=4,'ka_1'=2,'pts_0'=16,'pts_1'=4] {'pts_1'}, dimensions={2}, use_global_device_ids=true | all-gather | bytes 207360 | tf_op jit(solution)/shard_map/all_gather | solution.py:22
  19.8 8.5 %fusion.63 = (bf16[27,2,64,8]{3,2,1,0:T(8,128)(2,1)S(1)}, bf16[27,2,64,8]{3,2,1,0:T(8,128)(2,1)S(1)}, bf16[27,2,64,8]{3,2,1,0:T(8,128)(2,1)S(1)}, bf16[27,2,64,8...) fusion(bf16[27,2,64,64]{3,2,1,0:T(8,128)(2,1)} %param.7), kind=kLoop, calls=%fused_computation.85 | loop fusion | bytes 884736 | tf_op jit(solution)/shard_map/split | solution.py:15
  28.3 2.1 %copy.132 = bf16[27,2,64,8]{2,3,1,0:T(8,128)(2,1)} copy(bf16[27,2,64,8]{3,2,1,0:T(8,128)(2,1)} %get-tuple-element.16) | data formatting | bytes 110592
  30.4 2.1 %copy.133 = bf16[27,2,64,8]{2,3,1,0:T(8,128)(2,1)} copy(bf16[27,2,64,8]{3,2,1,0:T(8,128)(2,1)} %get-tuple-element.15) | data formatting | bytes 110592
  32.5 2.1 %copy.134 = bf16[27,2,64,8]{2,3,1,0:T(8,128)(2,1)} copy(bf16[27,2,64,8]{3,2,1,0:T(8,128)(2,1)} %get-tuple-element.14) | data formatting | bytes 110592
  34.6 2.1 %copy.135 = bf16[27,2,64,8]{2,3,1,0:T(8,128)(2,1)} copy(bf16[27,2,64,8]{3,2,1,0:T(8,128)(2,1)} %get-tuple-element.13) | data formatting | bytes 110592
  36.7 0.9 copy.136
  38.3 0.3 copy.139
  39.3 1.3 reshape.131
  40.7 11.8 %all-to-all-start = ((bf16[8,2,13824]{2,1,0:T(2,128)(2,1)}), bf16[8,2,13824]{2,1,0:T(2,128)(2,1)S(1)}, u32[]{:S(2)}, u32[]{:S(2)}) async-start(bf16[8,2,13824]{2,1,0:T(2,128)(2,1)} %reshape.131), calls=%async_computation | async-start | bytes 884736 | tf_op jit(solution)/shard_map/all_to_all | solution.py:16
  52.8 8.2 %all-to-all-done = bf16[8,2,13824]{2,1,0:T(2,128)(2,1)S(1)} async-done(((bf16[8,2,13824]{2,1,0:T(2,128)(2,1)}), bf16[8,2,13824]{2,1,0:T(2,128)(2,1)S(1)}, u32[]{:S(2)}, u32[]{:S(2)}) %all-to-all-start) | async-done | bytes 442400 | tf_op jit(solution)/shard_map/all_to_all | solution.py:16
  61.1 0.5 reshape.132
  61.6 4.8 %copy.67 = bf16[8,27,2,64,8]{4,3,2,1,0:T(8,128)(2,1)} copy(bf16[8,27,2,64,8]{3,4,2,1,0:T(8,128)(2,1)S(1)} %bitcast.176) | data formatting | bytes 884736 | tf_op jit(solution)/shard_map/all_to_all | solution.py:16
  66.4 9.7 %reshape.105 = bf16[6,6,6,2,512]{4,3,2,1,0:T(2,128)(2,1)S(1)} reshape(bf16[8,27,2,64,8]{4,3,2,1,0:T(8,128)(2,1)} %copy.67) | data formatting | bytes 884736 | tf_op jit(solution)/shard_map/reshape | solution.py:85
  76.2 0.8 convolution_bitcast_fusion.8
  77.0 16.0 %all-gather.2.cloned.1.call-done = bf16[27,2,64,384]{3,1,0,2:T(2,128)(2,1)} async-done(((bf16[27,2,4,384]{3,1,0,2:T(2,128)(2,1)}), bf16[27,2,64,384]{3,1,0,2:T(2,128)(2,1)}) %all-gather.2.cloned.1.call-update) | async-done | bytes 2654224 | tf_op jit(solution)/shard_map/all_gather | solution.py:22
  93.0 6.9 %fusion.62 = (bf16[27,1,64,384]{3,1,0,2:T(2,128)(2,1)S(1)}, bf16[27,1,64,384]{3,1,0,2:T(2,128)(2,1)S(1)}) fusion(bf16[27,2,64,384]{3,1,0,2:T(2,128)(2,1)} %all-gather.2.cloned.1.call-done), kind=kLoop, calls=%fused_computation.84 | loop fusion | bytes 5308416 | tf_op jit(solution)/shard_map/slice | solution.py:55
  99.9 0.6 fusion.1
  100.5 0.6 fusion.3
  101.1 0.6 fusion.26
  101.8 0.6 fusion.23
  102.6 0.8 copy.78
  103.4 1.3 reshape.129
  104.7 13.8 %all-to-all-start.1 = ((bf16[8,2,13824]{2,1,0:T(2,128)(2,1)}), bf16[8,2,13824]{2,1,0:T(2,128)(2,1)S(1)}, u32[]{:S(2)}, u32[]{:S(2)}) async-start(bf16[8,2,13824]{2,1,0:T(2,128)(2,1)} %reshape.129), calls=%async_computation.1 | async-start | bytes 884736 | tf_op jit(solution)/shard_map/all_to_all | solution.py:103
  118.5 1.9 convolution_bitcast_fusion.6
  120.4 1.8 convolution_bitcast_fusion.5
  122.2 5.0 %all-to-all-done.1 = bf16[8,2,13824]{2,1,0:T(2,128)(2,1)S(1)} async-done(((bf16[8,2,13824]{2,1,0:T(2,128)(2,1)}), bf16[8,2,13824]{2,1,0:T(2,128)(2,1)S(1)}, u32[]{:S(2)}, u32[]{:S(2)}) %all-to-all-start.1) | async-done | bytes 442400 | tf_op jit(solution)/shard_map/all_to_all | solution.py:103
  127.1 0.5 reshape.130
  127.9 4.8 %copy.80 = bf16[8,27,2,64,8]{4,3,2,1,0:T(8,128)(2,1)} copy(bf16[8,27,2,64,8]{3,4,0,2,1:T(8,128)(2,1)S(1)} %bitcast.175) | data formatting | bytes 884736 | tf_op jit(solution)/shard_map/all_to_all | solution.py:103
  132.7 9.9 %reshape.106 = bf16[6,6,6,2,512]{4,3,2,1,0:T(2,128)(2,1)S(1)} reshape(bf16[8,27,2,64,8]{4,3,2,1,0:T(8,128)(2,1)} %copy.80) | data formatting | bytes 884736 | tf_op jit(solution)/shard_map/reshape | solution.py:84
  142.6 0.8 convolution_bitcast_fusion.7
  143.5 1.9 convolution_bitcast_fusion.4
  145.3 1.8 convolution_bitcast_fusion.3
  147.5 1.8 convolution_bitcast_fusion.2
  149.3 1.9 convolution_bitcast_fusion.1
  151.2 1.7 fusion.22
  152.9 0.3 copy.89
  153.3 9.4 %convert_element_type.66 = bf16[4,2,27,2,64,8]{5,4,3,2,1,0:T(8,128)(2,1)} reshape(bf16[6,6,6,2,512]{4,3,2,1,0:T(2,128)(2,1)S(1)} %copy.89) | data formatting | bytes 884736 | tf_op jit(solution)/shard_map/convert_element_type | solution.py:90
  162.6 5.5 %copy.90 = bf16[4,2,27,2,64,8]{4,5,3,2,0,1:T(8,128)(2,1)S(1)} copy(bf16[4,2,27,2,64,8]{5,4,3,2,1,0:T(8,128)(2,1)} %convert_element_type.66) | data formatting | bytes 884736 | tf_op jit(solution)/shard_map/convert_element_type | solution.py:90
  168.1 0.8 reshape.133
  168.9 4.6 %all_to_all.30 = bf16[2,2,55296]{2,1,0:T(2,128)(2,1)S(1)} all-to-all(bf16[2,2,55296]{2,1,0:T(2,128)(2,1)S(1)} %reshape.133), channel_id=1, replica_groups=mesh['ka_0'=4,'ka_1'=2,'pts_0'=16,'pts_1'=4] {'ka_1'}, dimensions={0} | all-to-all | bytes 884736 | tf_op jit(solution)/shard_map/all_to_all | solution.py:41
  173.5 0.7 reshape.134
  174.3 0.5 reshape.135
  174.8 10.4 %all_to_all.31 = bf16[4,2,27648]{2,1,0:T(2,128)(2,1)S(1)} all-to-all(bf16[4,2,27648]{2,1,0:T(2,128)(2,1)S(1)} %reshape.135), channel_id=1, replica_groups=mesh['ka_0'=4,'ka_1'=2,'pts_0'=16,'pts_1'=4] {'ka_0'}, dimensions={0} | all-to-all | bytes 884736 | tf_op jit(solution)/shard_map/all_to_all | solution.py:41
  185.3 0.5 reshape.136
  186.0 1.2 copy.93
  (39 shorter events, 3.0 us)
Async XLA Ops:
  6.5 86.5 %all-gather.2.cloned.1.call-start = ((), (), s32[]{:S(2)}) async-start(), calls=%async_computation.4 | async-start | bytes 2820096 | tf_op jit(solution)/shard_map/all_gather | solution.py:22
  37.9 0.9 copy-start.3
  37.9 1.0 copy-start.4
  38.0 1.0 copy-start.2
  38.0 1.1 copy-start.1
  38.3 1.0 copy-start
  40.7 20.4 %all-to-all-start = ((bf16[8,2,13824]{2,1,0:T(2,128)(2,1)}), bf16[8,2,13824]{2,1,0:T(2,128)(2,1)S(1)}, u32[]{:S(2)}, u32[]{:S(2)}) async-start(bf16[8,2,13824]{2,1,0:T(2,128)(2,1)} %reshape.131), calls=%async_computation | async-start | bytes 884736 | tf_op jit(solution)/shard_map/all_to_all | solution.py:16
  93.0 6.9 %copy-start.5 = (bf16[27,2,64,384]{3,2,1,0:T(8,128)(2,1)S(1)}, bf16[27,2,64,384]{3,2,1,0:T(8,128)(2,1)}, u32[]{:S(2)}) copy-start(bf16[27,2,64,384]{3,2,1,0:T(8,128)(2,1)} %param.4) | copy-start | bytes 7962628
  104.7 22.4 %all-to-all-start.1 = ((bf16[8,2,13824]{2,1,0:T(2,128)(2,1)}), bf16[8,2,13824]{2,1,0:T(2,128)(2,1)S(1)}, u32[]{:S(2)}, u32[]{:S(2)}) async-start(bf16[8,2,13824]{2,1,0:T(2,128)(2,1)} %reshape.129), calls=%async_computation.1 | async-start | bytes 884736 | tf_op jit(solution)/shard_map/all_to_all | solution.py:103
Sparse Core Ops, SparseCore 0:
  19.9 73.0 all-gather.1
